TPU v7x, 128 devices: a whole 4x4x4 slice. The times are simulated.
128 devices in a mesh: samp: 16 (over y, z), feat: 8 (over x, core).
Axes of the slice: x: 4, y: 4, z: 4, core: 2. Of those that a mesh axis runs over, the one named last changes fastest.
Arguments:
- samples: bfloat16 [32768, 16384], P('samp', 'feat'), may hold values from -6 to 6
- residual_in: float32 [32768, 128], P('samp'), may hold values from -6 to 6
- weights_in: float32 [16384, 128], P('feat'), may hold values from -6 to 6
- inverses: float32 [8, 2048, 2048], P('feat', 'samp'), as said below
- order: int32 [6], replicated, may hold values from 0 to 7
Outputs:
- weights: float32 [16384, 128], P('feat')
- residual: float32 [32768, 128], P('samp')
Inputs may be any that keep to these rules, and one draw needn't show every extreme that they name: The inverses are full symmetric positive definite matrices; diagonal entries lie between 0.5 / 32768 and 2 / 32768, and off-diagonal entries are about 0.4 / sqrt(2048) of the diagonal scale.
All inputs are finite; a program needn't handle non-finite values.
Results may differ from a plain program's by a relative error of at most 0.009.
Values sent between devices are 32-bit elements; how exact they have to be, the bound alone decides.
A program may use at most 64 MiB of HBM per device.

v0:
```python
import jax
import jax.numpy as jnp
from jax import lax
from jax.sharding import PartitionSpec as P

STEPS = 6


def broadcast(value, axis, source):
    kept = jnp.where(lax.axis_index(axis) == source, value, 0).astype(value.dtype)
    return lax.psum(kept, axis)


def on_device(samples, residual_in, weights_in, inverses, order):
    penalty = samples.shape[0] * lax.axis_size("samp") / 64.0
    my_block = lax.axis_index("feat")
    weights = weights_in
    residual = residual_in
    inverse = inverses[0]
    for step in range(STEPS):
        block = order[step]
        owner = my_block == block
        grad = lax.dot_general(
            samples,
            residual.astype(jnp.bfloat16),
            (((0,), (0,)), ((), ())),
            preferred_element_type=jnp.float32,
        )
        grad = lax.psum(grad, "samp")
        grad = grad - penalty * weights
        my_rows = jnp.dot(
            inverse, grad, precision=lax.Precision.HIGHEST, preferred_element_type=jnp.float32
        )
        piece = lax.all_gather(my_rows, "samp", axis=0, tiled=True)
        updated = weights
        change = jnp.dot(samples, piece.astype(jnp.bfloat16), preferred_element_type=jnp.float32)
        old_rows = updated
        updated = old_rows + piece
        change, updated = (change, updated)
        weights = jnp.where(owner, updated, weights)
        change = broadcast(change, "feat", block)
        residual = residual - change
    return (weights, residual)


def solution(mesh):
    placed = (P("samp", "feat"), P("samp", None), P("feat", None), P("feat", "samp", None), P())
    return jax.shard_map(
        on_device,
        mesh=mesh,
        in_specs=placed,
        out_specs=(P("feat", None), P("samp", None)),
        check_vma=False,
    )
```

profile of v0, /device:TPU:1, one launch (start us, length us, event | category | flops | bytes accessed | tf_op | source)
XLA Modules:
  0.0 1274.4 jit_solution(6375994803973724864)
XLA Ops:
  14.9 87.4 %all-reduce.13.cloned.1.call-done = f32[2048,128]{0,1:T(8,128)} async-done(((f32[2048,128]{0,1:T(8,128)}), f32[2048,128]{0,1:T(8,128)}) %all-reduce.13.cloned.1.call-update) | async-done | bytes 1048592 | tf_op jit(solution)/shard_map/psum | solution.py:29
  106.7 41.4 %all-gather.7.cloned.1.call-done = f32[2048,128]{0,1:T(8,128)} async-done(((f32[128,128]{0,1:T(8,128)}), f32[2048,128]{0,1:T(8,128)}) %all-gather.7.cloned.1.call-update) | async-done | bytes 1048592 | tf_op jit(solution)/shard_map/all_gather | solution.py:34
  148.1 7.6 fusion.5
  157.1 59.7 %all-reduce.15.cloned.1.call-done = f32[2048,128]{0,1:T(8,128)} async-done(((f32[2048,128]{0,1:T(8,128)}), f32[2048,128]{0,1:T(8,128)}) %all-reduce.15.cloned.1.call-update) | async-done | bytes 1048592 | tf_op jit(solution)/shard_map/psum | solution.py:11
  224.1 87.2 %all-reduce.17.cloned.1.call-done = f32[2048,128]{0,1:T(8,128)} async-done(((f32[2048,128]{0,1:T(8,128)}), f32[2048,128]{0,1:T(8,128)}) %all-reduce.17.cloned.1.call-update) | async-done | bytes 1048592 | tf_op jit(solution)/shard_map/psum | solution.py:29
  315.3 42.2 %all-gather.9.cloned.1.call-done = f32[2048,128]{0,1:T(8,128)} async-done(((f32[128,128]{0,1:T(8,128)}), f32[2048,128]{0,1:T(8,128)}) %all-gather.9.cloned.1.call-update) | async-done | bytes 1048592 | tf_op jit(solution)/shard_map/all_gather | solution.py:34
  357.5 7.6 fusion.4
  365.1 61.0 %all-reduce.19.cloned.1.call-done = f32[2048,128]{0,1:T(8,128)} async-done(((f32[2048,128]{0,1:T(8,128)}), f32[2048,128]{0,1:T(8,128)}) %all-reduce.19.cloned.1.call-update) | async-done | bytes 1048592 | tf_op jit(solution)/shard_map/psum | solution.py:11
  436.1 85.2 %all-reduce.21.cloned.1.call-done = f32[2048,128]{0,1:T(8,128)} async-done(((f32[2048,128]{0,1:T(8,128)}), f32[2048,128]{0,1:T(8,128)}) %all-reduce.21.cloned.1.call-update) | async-done | bytes 1048592 | tf_op jit(solution)/shard_map/psum | solution.py:29
  525.0 42.1 %all-gather.11.cloned.1.call-done = f32[2048,128]{0,1:T(8,128)} async-done(((f32[128,128]{0,1:T(8,128)}), f32[2048,128]{0,1:T(8,128)}) %all-gather.11.cloned.1.call-update) | async-done | bytes 1048592 | tf_op jit(solution)/shard_map/all_gather | solution.py:34
  567.1 7.6 fusion.3
  574.8 61.0 %all-reduce.23.cloned.1.call-done = f32[2048,128]{0,1:T(8,128)} async-done(((f32[2048,128]{0,1:T(8,128)}), f32[2048,128]{0,1:T(8,128)}) %all-reduce.23.cloned.1.call-update) | async-done | bytes 1048592 | tf_op jit(solution)/shard_map/psum | solution.py:11
  643.9 87.2 %all-reduce.25.cloned.1.call-done = f32[2048,128]{0,1:T(8,128)} async-done(((f32[2048,128]{0,1:T(8,128)}), f32[2048,128]{0,1:T(8,128)}) %all-reduce.25.cloned.1.call-update) | async-done | bytes 1048592 | tf_op jit(solution)/shard_map/psum | solution.py:29
  735.0 42.2 %all-gather.13.cloned.1.call-done = f32[2048,128]{0,1:T(8,128)} async-done(((f32[128,128]{0,1:T(8,128)}), f32[2048,128]{0,1:T(8,128)}) %all-gather.13.cloned.1.call-update) | async-done | bytes 1048592 | tf_op jit(solution)/shard_map/all_gather | solution.py:34
  777.2 7.6 fusion.2
  784.8 61.0 %all-reduce.27.cloned.1.call-done = f32[2048,128]{0,1:T(8,128)} async-done(((f32[2048,128]{0,1:T(8,128)}), f32[2048,128]{0,1:T(8,128)}) %all-reduce.27.cloned.1.call-update) | async-done | bytes 1048592 | tf_op jit(solution)/shard_map/psum | solution.py:11
  855.7 85.4 %all-reduce.29.cloned.1.call-done = f32[2048,128]{0,1:T(8,128)} async-done(((f32[2048,128]{0,1:T(8,128)}), f32[2048,128]{0,1:T(8,128)}) %all-reduce.29.cloned.1.call-update) | async-done | bytes 1048592 | tf_op jit(solution)/shard_map/psum | solution.py:29
  944.9 41.9 %all-gather.15.cloned.1.call-done = f32[2048,128]{0,1:T(8,128)} async-done(((f32[128,128]{0,1:T(8,128)}), f32[2048,128]{0,1:T(8,128)}) %all-gather.15.cloned.1.call-update) | async-done | bytes 1048592 | tf_op jit(solution)/shard_map/all_gather | solution.py:34
  986.9 7.6 fusion.1
  994.5 61.0 %all-reduce.31.cloned.1.call-done = f32[2048,128]{0,1:T(8,128)} async-done(((f32[2048,128]{0,1:T(8,128)}), f32[2048,128]{0,1:T(8,128)}) %all-reduce.31.cloned.1.call-update) | async-done | bytes 1048592 | tf_op jit(solution)/shard_map/psum | solution.py:11
  1062.9 87.2 %all-reduce.33.cloned.1.call-done = f32[2048,128]{0,1:T(8,128)} async-done(((f32[2048,128]{0,1:T(8,128)}), f32[2048,128]{0,1:T(8,128)}) %all-reduce.33.cloned.1.call-update) | async-done | bytes 1048592 | tf_op jit(solution)/shard_map/psum | solution.py:29
  1154.0 42.2 %all-gather.17.cloned.1.call-done = f32[2048,128]{0,1:T(8,128)} async-done(((f32[128,128]{0,1:T(8,128)}), f32[2048,128]{0,1:T(8,128)}) %all-gather.17.cloned.1.call-update) | async-done | bytes 1048592 | tf_op jit(solution)/shard_map/all_gather | solution.py:34
  1196.2 7.6 fusion
  1209.1 55.8 %all-reduce.35.cloned.1.call-done = f32[2048,128]{0,1:T(8,128)} async-done(((f32[2048,128]{0,1:T(8,128)}), f32[2048,128]{0,1:T(8,128)}) %all-reduce.35.cloned.1.call-update) | async-done | bytes 1048592 | tf_op jit(solution)/shard_map/psum | solution.py:11
  (78 shorter events, 79.5 us)
Async XLA Ops:
  7.2 95.2 %copy-start = (f32[1,128,2048]{2,1,0:T(8,128)S(1)}, f32[1,128,2048]{2,1,0:T(8,128)}, u32[]{:S(2)}) copy-start(f32[1,128,2048]{2,1,0:T(8,128)} %param.8) | copy-start | bytes 3145732
  7.2 98.1 %copy-start.7 = (s32[6]{0:T(128)S(1)}, s32[6]{0:T(128)}, u32[]{:S(2)}) copy-start(s32[6]{0:T(128)} %param.9) | copy-start | bytes 76
  7.2 95.1 %all-reduce.13.cloned.1.call-start = ((), (), s32[]{:S(2)}) async-start(), calls=%async_computation | async-start | bytes 2097152 | tf_op jit(solution)/shard_map/psum | solution.py:29
  13.2 142.5 %copy-start.6 = (f32[2048,128]{1,0:T(8,128)S(1)}, f32[2048,128]{1,0:T(8,128)}, u32[]{:S(2)}) copy-start(f32[2048,128]{1,0:T(8,128)} %param.6) | copy-start | bytes 3145732
  13.3 134.9 %all-gather.7.cloned.1.call-start = ((), (), s32[]{:S(2)}) async-start(), calls=%async_computation.1 | async-start | bytes 1114112 | tf_op jit(solution)/shard_map/all_gather | solution.py:34
  105.3 111.5 %all-reduce.15.cloned.1.call-start = ((), (), s32[]{:S(2)}) async-start(), calls=%async_computation.2 | async-start | bytes 2097152 | tf_op jit(solution)/shard_map/psum | solution.py:11
  155.7 155.6 %all-reduce.17.cloned.1.call-start = ((), (), s32[]{:S(2)}) async-start(), calls=%async_computation.3 | async-start | bytes 2097152 | tf_op jit(solution)/shard_map/psum | solution.py:29
  224.1 133.4 %all-gather.9.cloned.1.call-start = ((), (), s32[]{:S(2)}) async-start(), calls=%async_computation.4 | async-start | bytes 1114112 | tf_op jit(solution)/shard_map/all_gather | solution.py:34
  314.6 111.5 %all-reduce.19.cloned.1.call-start = ((), (), s32[]{:S(2)}) async-start(), calls=%async_computation.5 | async-start | bytes 2097152 | tf_op jit(solution)/shard_map/psum | solution.py:11
  365.1 156.3 %all-reduce.21.cloned.1.call-start = ((), (), s32[]{:S(2)}) async-start(), calls=%async_computation.6 | async-start | bytes 2097152 | tf_op jit(solution)/shard_map/psum | solution.py:29
  434.1 133.0 %all-gather.11.cloned.1.call-start = ((), (), s32[]{:S(2)}) async-start(), calls=%async_computation.7 | async-start | bytes 1114112 | tf_op jit(solution)/shard_map/all_gather | solution.py:34
  436.1 199.7 %copy-start.2 = (f32[2048,128]{0,1:T(8,128)S(1)}, f32[2048,128]{0,1:T(8,128)}, u32[]{:S(2)}) copy-start(f32[2048,128]{0,1:T(8,128)} %copy-done.1) | copy-start | bytes 3145732
  524.3 111.5 %all-reduce.23.cloned.1.call-start = ((), (), s32[]{:S(2)}) async-start(), calls=%async_computation.8 | async-start | bytes 2097152 | tf_op jit(solution)/shard_map/psum | solution.py:11
  574.7 156.3 %all-reduce.25.cloned.1.call-start = ((), (), s32[]{:S(2)}) async-start(), calls=%async_computation.9 | async-start | bytes 2097152 | tf_op jit(solution)/shard_map/psum | solution.py:29
  637.1 1.0 copy-start.4
  643.8 202.1 %copy-start.5 = (f32[2048,128]{0,1:T(8,128)S(1)}, f32[2048,128]{0,1:T(8,128)}, u32[]{:S(2)}) copy-start(f32[2048,128]{0,1:T(8,128)} %copy-done.4) | copy-start | bytes 3145732
  643.8 133.4 %all-gather.13.cloned.1.call-start = ((), (), s32[]{:S(2)}) async-start(), calls=%async_computation.10 | async-start | bytes 1114112 | tf_op jit(solution)/shard_map/all_gather | solution.py:34
  734.4 111.5 %all-reduce.27.cloned.1.call-start = ((), (), s32[]{:S(2)}) async-start(), calls=%async_computation.11 | async-start | bytes 2097152 | tf_op jit(solution)/shard_map/psum | solution.py:11
  784.8 156.3 %all-reduce.29.cloned.1.call-start = ((), (), s32[]{:S(2)}) async-start(), calls=%async_computation.12 | async-start | bytes 2097152 | tf_op jit(solution)/shard_map/psum | solution.py:29
  853.9 133.0 %all-gather.15.cloned.1.call-start = ((), (), s32[]{:S(2)}) async-start(), calls=%async_computation.13 | async-start | bytes 1114112 | tf_op jit(solution)/shard_map/all_gather | solution.py:34
  944.0 111.5 %all-reduce.31.cloned.1.call-start = ((), (), s32[]{:S(2)}) async-start(), calls=%async_computation.14 | async-start | bytes 2097152 | tf_op jit(solution)/shard_map/psum | solution.py:11
  994.5 155.6 %all-reduce.33.cloned.1.call-start = ((), (), s32[]{:S(2)}) async-start(), calls=%async_computation.15 | async-start | bytes 2097152 | tf_op jit(solution)/shard_map/psum | solution.py:29
  1062.8 133.4 %all-gather.17.cloned.1.call-start = ((), (), s32[]{:S(2)}) async-start(), calls=%async_computation.16 | async-start | bytes 1114112 | tf_op jit(solution)/shard_map/all_gather | solution.py:34
  1153.4 111.5 %all-reduce.35.cloned.1.call-start = ((), (), s32[]{:S(2)}) async-start(), calls=%async_computation.17 | async-start | bytes 2097152 | tf_op jit(solution)/shard_map/psum | solution.py:11
  (2 other events, 1.9 us)
Sparse Core Ops, SparseCore 0:
  13.4 88.9 all-reduce.12
  105.4 42.6 all-gather.6
  155.8 60.8 all-reduce.14
  224.2 87.0 all-reduce.16
  314.7 42.6 all-gather.8
  365.2 60.8 all-reduce.18
  434.3 87.0 all-reduce.20
  524.4 42.6 all-gather.10
  574.9 60.8 all-reduce.22
  643.9 87.0 all-reduce.24
  734.5 42.6 all-gather.12
  784.9 60.9 all-reduce.26
  854.0 87.0 all-reduce.28
  944.1 42.6 all-gather.14
  994.6 60.8 all-reduce.30
  1062.9 87.0 all-reduce.32
  1153.5 42.6 all-gather.16
  1203.9 60.8 all-reduce.34
where the time goes:
time: 1280 us; the launch traced here: 1270 us
  waiting for transfers between devices  1130 us (88%)
  matrix products  98.3 us (8%)
  between operations  18.2 us (1%)
  other arithmetic  14.9 us (1%)
    psum x6, waiting for transfers between devices, on_device(): grad = lax.psum(grad, 'samp')  520 us
    psum x6, waiting for transfers between devices, broadcast(): return lax.psum(kept, axis)  360 us
    all_gather x6, waiting for transfers between devices, on_device(): piece = lax.all_gather(my_rows, 'samp', axis=0, tiled=True)  252 us
    dot_general x6, matrix products, on_device(): jnp.dot(samples, piece.astype(jnp.bfloat16), preferred_element_type=jnp.f...  45.5 us
    dot_general x6, matrix products, on_device(): lax.dot_general(samples, residual.astype(jnp.bfloat16), (((0,), (0,)), ((...  34.2 us
  transfers between devices with their start and end apart: 18, of which 18 were waited for; matrix products, arithmetic and copies ran while one was open for 1% of the time, Pallas kernels for 0%

commit v1 on v0

v1 whole, which is shorter than its diff:
```python
import functools

import jax
import jax.numpy as jnp
from jax import lax
from jax.experimental import pallas as pl
from jax.experimental.pallas import tpu as pltpu
from jax.sharding import PartitionSpec as P

STEPS = 6
STREAMS = 4
FAR_FIRST = (2, 1, 3)
PIECES = 16
MESH = pl.DeviceIdType.MESH
F32 = jnp.float32
BF16 = jnp.bfloat16

M_RS = 0
M_AR = 2
M_DP = 4
M_AG = 6
M_X1 = 8
M_X2 = 10
N_SEM = 12
CHUNKS = 1


def nn(a, b):
    return jnp.dot(a, b, preferred_element_type=F32)


def nt(a, b):
    return lax.dot_general(a, b, (((1,), (1,)), ((), ())), preferred_element_type=F32)


def kernel(
    penalty, order_ref, x_hbm, r_hbm, w_hbm, inv_hbm, r, w, r_in, w_in, inv_in,
    x_buf, xb, xs, xr, rs, rb, rb0, gp, rsb, ao, arb, dpb, d_buf, cm, x1, x1s, x2,
    cs, cr, bf, bh, load_sem, ssem, rsem, isend, irecv, osend, orecv, csend, crecv,
):
    streams, stream, rows = rb.shape
    feats = w.shape[2]
    half, quarter = stream // 2, stream // 4
    blk, rblk = feats // 4, rows // CHUNKS
    k = lax.axis_index("samp")
    f = lax.axis_index("feat")
    y, z = k // 4, k % 4
    x, core = f // 2, f % 2
    other = x * 2 + 1 - core
    sib = (k, other)

    def zdev(t, feat=f):
        return (y * 4 + t, feat)

    def ydev(t, feat=f):
        return (t * 4 + z, feat)

    xdev = [(k, (x + 1 - 2 * (x % 2)) * 2 + core), (k, (3 - x) * 2 + core)]
    first = [(z, zdev), (y, ydev)]
    second = [(y, ydev), (z, zdev)]

    def at(pos, size):
        return pl.ds(pl.multiple_of(pos * size, size), size)

    def outs_of(core_of, q):
        return pl.ds(pl.multiple_of(core_of * half + q * quarter, quarter), quarter)

    def hrows(q):
        return pl.ds(q * half, half)

    def load(src, dst, i):
        c = pltpu.make_async_copy(src, dst, load_sem.at[i])
        c.start()
        return c

    inv_load = load(inv_hbm, inv_in, 5)
    r_load = load(r_hbm, r_in, 6)
    loads = []
    for b in range(4):
        cols = pl.ds(b * blk, blk)
        loads.append(load(x_hbm.at[:, cols], x_buf.at[:, cols], b))
    w_load = load(w_hbm, w_in, 7)

    barrier = pltpu.get_barrier_semaphore()
    partners = [sib, xdev[0], xdev[1]]
    for d in (1, 2, 3):
        for feat in (f, other):
            partners += [zdev((z + d) % 4, feat), ydev((y + d) % 4, feat)]
    for dev in partners:
        pl.semaphore_signal(barrier, inc=1, device_id=dev, device_id_type=MESH)

    r_load.wait()
    turned = r_in[...].T
    r[...] = turned.reshape(r.shape)
    rb0[...] = turned.astype(BF16)
    pl.semaphore_wait(barrier, len(partners))

    def inv_copy(d, src, dst, dev):
        return pltpu.make_async_remote_copy(src, dst, isend.at[d], irecv.at[d], dev, MESH)

    def inv_piece(core_of, d):
        return bf.at[core_of, at((z + 4 - d) % 4, blk // 4)]

    inv_load.wait()
    for d in (1, 2, 3):
        t = (z + d) % 4
        inv_copy(d, inv_in.at[:, at(t, blk)], inv_piece(core, 0), zdev(t)).start()
    bf[core, at(z, blk // 4)] = inv_in[:, at(z, blk)]
    inv_copy(4, inv_piece(core, 0), inv_piece(core, 0), sib).start()


    mine = at(core, rows)
    its = at(1 - core, rows)

    piece = rows // PIECES

    def half_copy(b):
        part = at(b, piece)
        return pltpu.make_async_remote_copy(xs.at[part], xr.at[part], osend.at[b], orecv.at[b], sib, MESH)

    def send_half(b):
        here = pl.ds(pl.multiple_of((1 - core) * rows + b * piece, piece), piece)
        xs[at(b, piece)] = x_buf[here].astype(F32)
        half_copy(b).start()

    def take_half(b):
        half_copy(b).wait()
        xb[1 - core, at(b, piece)] = xr[at(b, piece)].astype(BF16)

    class Step:
        def __init__(self, t):
            self.u, self.s = lax.rem(t, streams), t // streams
            self.slot = lax.rem(self.s, 2)
            self.order = order_ref[self.s]
            self.parity = lax.rem(self.order, 2)
            self.own = jnp.where(self.order == f, 1.0, 0.0).astype(F32)
            self.near = jnp.where(self.order - self.parity == 2 * x, 1.0, 0.0).astype(F32)

        def copy(self, num, src, dst, dev):
            here = self.u, self.slot
            return pltpu.make_async_remote_copy(src, dst, ssem.at[here], rsem.at[(*here, num)], dev, MESH)

        def send(self, num, src, dst, dev):
            self.copy(num, src, dst, dev).start()

        def arrived(self, num, dst):
            self.copy(num, dst, dst, sib).wait_recv()

        def all_left(self):
            sent = xr.at[pl.ds(0, (40 * quarter * blk + 2 * stream * rows) // feats)]
            self.copy(0, sent, sent, sib).wait_send()

        def gradient(self):
            u, slot = self.u, self.slot
            for pair in (1 - z // 2, z // 2):
                cols = at(pair, 2 * blk)
                g = nn(rb[u], xb[self.parity, :, cols])
                gp[u, :, cols] = self.near * g - self.own * penalty * w[u, :, cols]
                for b in (pair * 2, pair * 2 + 1):
                    cols = at(b, blk)
                    d = (b + 4 - z) % 4
                    self.send(M_RS, gp.at[u, outs_of(1 - core, 0), cols], rsb.at[u, slot, 0, 3 + d], zdev(b, other))
                    d = (b + 4 - y) % 4
                    self.send(M_RS + 1, gp.at[u, outs_of(1 - core, 1), cols], rsb.at[u, slot, 1, 3 + d], ydev(b, other))
            for d in FAR_FIRST:
                b = (z + d) % 4
                self.send(M_RS, gp.at[u, outs_of(core, 0), at(b, blk)], rsb.at[u, slot, 0, d - 1], zdev(b))
                b = (y + d) % 4
                self.send(M_RS + 1, gp.at[u, outs_of(core, 1), at(b, blk)], rsb.at[u, slot, 1, d - 1], ydev(b))

        def scatter(self, b, value):
            u, slot = self.u, self.slot
            cols = pl.ds(b * blk, blk)
            gp[u, :, cols] = value
            for q in range(2):
                pos, dev = first[q]
                d = (b + 4 - pos) % 4
                self.send(
                    M_RS + q, gp.at[u, outs_of(1 - core, q), cols], rsb.at[u, slot, q, 3 + d], dev(b, other)
                )

                @pl.when(d != 0)
                def _():
                    self.send(M_RS + q, gp.at[u, outs_of(core, q), cols], rsb.at[u, slot, q, d - 1], dev(b))

        def reduce(self):
            u, slot = self.u, self.slot
            for q in range(2):
                self.arrived(M_RS + q, rsb.at[u, slot, q])
                acc = gp[u, outs_of(core, q), at(first[q][0], blk)]
                for i in range(7):
                    acc = acc + rsb[u, slot, q, i]
                ao[u, q] = acc
                pos, dev = second[q]
                for d in FAR_FIRST:
                    self.send(M_AR + q, ao.at[u, q], arb.at[u, slot, q, d - 1], dev((pos + d) % 4))

        def multiply(self):
            u, slot = self.u, self.slot
            for q in range(2):
                self.arrived(M_AR + q, arb.at[u, slot, q])
                acc = ao[u, q] + arb[u, slot, q, 0] + arb[u, slot, q, 1] + arb[u, slot, q, 2]
                hi = acc.astype(BF16).astype(F32)
                both = jnp.concatenate([hi, acc - hi], axis=0).astype(BF16)
                dot = nt if q == 0 else nn
                whole = dot(both, bh[self.parity])
                pos, dev = first[q]
                dpb[u, slot, q, pos] = whole[:quarter] + whole[quarter:]
                here = dpb.at[u, slot, q, pos]
                for d in FAR_FIRST:
                    self.send(M_DP + q, here, here, dev((pos + d) % 4))

        def gather(self):
            u, slot = self.u, self.slot
            for q in range(2):
                self.arrived(M_DP + q, arb.at[u, slot, q])
                pos, dev = second[q]
                here = d_buf.at[u, slot, outs_of(core, q), at(pos, blk)]
                here[...] = (dpb[u, slot, q, 0] + dpb[u, slot, q, 1]) + (dpb[u, slot, q, 2] + dpb[u, slot, q, 3])
                for d in FAR_FIRST:
                    for feat in (f, other):
                        self.send(M_AG + q, here, here, dev((pos + d) % 4, feat))
                self.send(M_AG + q, here, here, sib)

        def gathered(self):
            u, slot = self.u, self.slot
            for q in range(2):
                self.arrived(M_AG + q, rsb.at[u, slot, q])
            w[u] += self.own * d_buf[u, slot]

        def change(self):
            db = d_buf[self.u, self.slot].astype(BF16)
            for b in range(CHUNKS):
                self.exchange(b, self.near * nt(db, xb[self.parity, pl.ds(b * rblk, rblk), :]))

        def merge(self, b):
            here = (self.u, slice(None), pl.ds(b * rblk, rblk))
            sems = csend.at[self.u, b], crecv.at[self.u, b]
            return pltpu.make_async_remote_copy(cs.at[here], cr.at[here], *sems, sib, MESH)

        def first_change(self):
            u, slot = self.u, self.slot
            db = d_buf[u, slot].astype(BF16)

            def part(core_of, b):
                here = pl.ds(pl.multiple_of(core_of * rows + b * rblk, rblk), rblk)
                return self.own * nt(db, x_buf[here, :])

            for b in range(CHUNKS):
                cs[u, :, pl.ds(b * rblk, rblk)] = part(1 - core, b)
                self.merge(b).start()
            for b in range(CHUNKS):
                cm[u, :, pl.ds(b * rblk, rblk)] = part(core, b)

        def first_merge(self):
            for b in range(CHUNKS):
                cols = pl.ds(b * rblk, rblk)
                self.merge(b).wait()
                self.exchange(b, cm[self.u, :, cols] + cr[self.u, :, cols])

        def exchange(self, b, value):
            u, slot = self.u, self.slot
            cols = pl.ds(b * rblk, rblk)
            cm[u, :, cols] = value
            for q in range(2):
                self.send(M_X1 + b, cm.at[u, hrows(q), cols], x1.at[u, slot, hrows(q), cols], xdev[q])

        def exchange2(self):
            u, slot = self.u, self.slot
            for b in range(CHUNKS):
                cols = pl.ds(b * rblk, rblk)
                self.arrived(M_X1 + b, x1.at[u, slot, :, cols])
                x1s[u, :, cols] = cm[u, :, cols] + x1[u, slot, :, cols]
                for q in range(2):
                    self.send(M_X2 + b, x1s.at[u, hrows(q), cols], x2.at[u, slot, hrows(q), cols], xdev[1 - q])

        def total(self):
            u, slot = self.u, self.slot
            for b in range(CHUNKS):
                cols = pl.ds(b * rblk, rblk)
                here = (u, slice(None), pl.ds(pl.multiple_of(core * rows + b * rblk, rblk), rblk))
                self.arrived(M_X2 + b, x2.at[u, slot, :, cols])
                new = r[here] - (x1s[u, :, cols] + x2[u, slot, :, cols])
                r[here] = new
                rb[u, :, cols] = new.astype(BF16)

    def give_rows(u):
        sems = osend.at[PIECES + u], orecv.at[PIECES + u]
        return pltpu.make_async_remote_copy(r.at[u, :, mine], r.at[u, :, mine], *sems, sib, MESH)

    steps = [Step(jnp.int32(u)) for u in range(streams)]
    for b in range(4):
        cols = pl.ds(b * blk, blk)
        loads[b].wait()
        if b == 0:
            w_load.wait()
        w[:, :, cols] = w_in[cols, :].T.reshape(streams, stream, blk)
        g = nn(rb0[...], x_buf[:, cols])
        for u in range(streams):
            part = g[u * stream:(u + 1) * stream]
            steps[u].scatter(b, steps[u].own * (part - penalty * w[u, :, cols]))
    for b in range(5):
        send_half(b)
    for d in (1, 3, 2):
        here = inv_piece(core, d)
        inv_copy(d, here, here, sib).wait()
        inv_copy(4 + d, here, here, sib).start()
    for b in range(5, 10):
        send_half(b)
    own_half = load(x_hbm.at[at(core, rows)], xb.at[core], 4)

    starts = STEPS * streams

    def quarter_step(t, carry, edge):
        def when(lo, hi, part):
            if edge:
                pl.when((t >= lo) & (t < hi))(part)
            else:
                part()

        a, b, c, d = (Step(jnp.clip(t - i, 0, starts - 1)) for i in range(4))
        if edge:
            when(streams, starts, a.gradient)
        else:
            a.gradient()
        when(3, starts + 3, d.exchange2)
        when(1, starts + 1, b.multiply)
        when(2, starts + 2, c.gathered)
        if edge:
            when(2, streams + 2, c.first_change)
        when(streams + 2, starts + 2, c.change)
        when(0, starts, a.reduce)
        if edge:
            when(2, streams + 2, c.first_merge)
        when(1, starts + 1, b.gather)
        when(3, starts + 3, d.total)
        when(3, starts + 3, d.all_left)
        return carry

    def take_inverse():
        for d in range(4):
            inv_copy(4 + d, inv_piece(core, d), inv_piece(core, d), sib).wait_send()
            inv_copy(4 + d, inv_piece(1 - core, d), inv_piece(1 - core, d), sib).wait_recv()
        for o in range(2):
            bh[o] = bf[o].astype(BF16)

    def take_samples(lo, hi):
        def take(b, carry):
            take_half(b)
            return carry

        lax.fori_loop(lo, hi, take, 0)

    def first_quarter_step(t, carry):
        pl.when(t == 1)(take_inverse)
        pl.when(t == streams)(own_half.wait)
        pl.when(t == streams)(functools.partial(take_samples, 9, PIECES))
        quarter_step(t, carry, True)
        pl.when(t == 2)(functools.partial(take_samples, 0, 5))
        pl.when(t == 3)(functools.partial(take_samples, 5, 9))

        @pl.when(t < 3)
        def _():
            for i in range(2):
                send_half(10 + t * 2 + i)

        return carry

    def last_quarter_step(t, carry):
        quarter_step(t, carry, True)
        give_rows(lax.rem(t - 3, streams)).start()
        return carry

    lax.fori_loop(0, streams + 2, first_quarter_step, 0)
    lax.fori_loop(streams + 2, starts - 1, functools.partial(quarter_step, edge=False), 0)
    lax.fori_loop(starts - 1, starts + 3, last_quarter_step, 0)
    for u in range(streams):
        there = r.at[u, :, its]
        sems = osend.at[PIECES + u], orecv.at[PIECES + u]
        give_rows(u).wait_send()
        pltpu.make_async_remote_copy(there, there, *sems, sib, MESH).wait_recv()


def on_device(samples, residual_in, weights_in, inverses, order):
    chip_rows, feats = samples.shape
    outs = residual_in.shape[1]
    rows = chip_rows // 2
    stream = outs // STREAMS
    quarter = stream // 4
    blk = feats // 4
    samp = lax.axis_size("samp")
    penalty = chip_rows * samp / 64.0 / samp
    vmem = pl.BlockSpec(memory_space=pltpu.VMEM)
    smem = pl.BlockSpec(memory_space=pltpu.SMEM)
    per_rows = (STREAMS, stream, rows)
    per_chip = (STREAMS, stream, chip_rows)
    per_feats = (STREAMS, stream, feats)
    residual, weights = pl.pallas_call(
        functools.partial(kernel, penalty),
        out_shape=[jax.ShapeDtypeStruct(per_chip, F32), jax.ShapeDtypeStruct(per_feats, F32)],
        in_specs=[smem] + [pl.BlockSpec(memory_space=pl.ANY)] * 4,
        out_specs=[vmem, vmem],
        scratch_shapes=[
            pltpu.VMEM((chip_rows, outs), F32),
            pltpu.VMEM((feats, outs), F32),
            pltpu.VMEM((blk // 4, feats), F32),
            pltpu.VMEM((chip_rows, feats), BF16),
            pltpu.VMEM((2, rows, feats), BF16),
            pltpu.VMEM((rows, feats), F32),
            pltpu.VMEM((rows, feats), F32),
            pltpu.VMEM(per_rows, F32),
            pltpu.VMEM(per_rows, BF16),
            pltpu.VMEM((outs, chip_rows), BF16),
            pltpu.VMEM(per_feats, F32),
            pltpu.VMEM((STREAMS, 2, 2, 7, quarter, blk), F32),
            pltpu.VMEM((STREAMS, 2, quarter, blk), F32),
            pltpu.VMEM((STREAMS, 2, 2, 3, quarter, blk), F32),
            pltpu.VMEM((STREAMS, 2, 2, 4, quarter, blk), F32),
            pltpu.VMEM((STREAMS, 2, stream, feats), F32),
            pltpu.VMEM(per_rows, F32),
            pltpu.VMEM((STREAMS, 2, stream, rows), F32),
            pltpu.VMEM(per_rows, F32),
            pltpu.VMEM((STREAMS, 2, stream, rows), F32),
            pltpu.VMEM(per_rows, F32),
            pltpu.VMEM(per_rows, F32),
            pltpu.VMEM((2, blk, blk), F32),
            pltpu.VMEM((2, blk, blk), BF16),
            pltpu.SemaphoreType.DMA((8,)),
            pltpu.SemaphoreType.DMA((STREAMS, 2)),
            pltpu.SemaphoreType.DMA((STREAMS, 2, N_SEM)),
            pltpu.SemaphoreType.DMA((8,)),
            pltpu.SemaphoreType.DMA((8,)),
            pltpu.SemaphoreType.DMA((PIECES + STREAMS,)),
            pltpu.SemaphoreType.DMA((PIECES + STREAMS,)),
            pltpu.SemaphoreType.DMA((STREAMS, CHUNKS)),
            pltpu.SemaphoreType.DMA((STREAMS, CHUNKS)),
        ],
        compiler_params=pltpu.CompilerParams(
            collective_id=0, has_side_effects=True, vmem_limit_bytes=56 * 1024 * 1024
        ),
        cost_estimate=pl.CostEstimate(
            flops=STEPS * 4 * rows * feats * outs, bytes_accessed=2 * chip_rows * feats, transcendentals=0
        ),
    )(order, samples, residual_in, weights_in, inverses[0])
    return weights.reshape(outs, feats).T, residual.reshape(outs, chip_rows).T


def solution(mesh):
    placed = (P("samp", "feat"), P("samp", None), P("feat", None), P("feat", "samp", None), P())
    return jax.shard_map(
        on_device,
        mesh=mesh,
        in_specs=placed,
        out_specs=(P("feat", None), P("samp", None)),
        check_vma=False,
    )
```

time: 1280 us -> 215 us (0.17)
  waiting for transfers between devices: 1130 us -> 0 us
  Pallas kernels: 0 us -> 210 us
  matrix products: 98.3 us -> 0 us
  between operations: 18.2 us -> 0.64 us
  other arithmetic: 14.9 us -> 0 us
    psum x12 -> x0, waiting for transfers between devices: 879 us -> none  [the longest x6 520 us: on_device(): grad = lax.psum(grad, 'samp')]
    all_gather x6 -> x0, waiting for transfers between devices: 252 us -> none  [on_device(): piece = lax.all_gather(my_rows, 'samp', axis=0, tiled=True)]
    pallas_call x0 -> x1, Pallas kernels: none -> 210 us  [on_device(): pl.pallas_call(functools.partial(kernel, penalty), out_shape=[jax.ShapeDt...]
    dot_general x18 -> x0, matrix products: 98.3 us -> none  [the longest x6 45.5 us: on_device(): jnp.dot(samples, piece.astype(jnp.bfloat16), preferred_element_type=jnp.f...]
  transfers between devices with their start and end apart: 18 -> 0, of which waited for: 18 -> 0; matrix products, arithmetic and copies ran while one was open for 1% -> 0% of each run, Pallas kernels for 0% -> 0%
where the time goes in v1:
time: 215 us
  Pallas kernels  210 us (98%)
  local copies, waits for them, and re-layouts  5.06 us (2%)
    pallas_call x1, Pallas kernels, on_device(): pl.pallas_call(functools.partial(kernel, penalty), out_shape=[jax.ShapeDt...  210 us
    reshape x2, local copies, waits for them, and re-layouts, on_device(): return (weights.reshape(outs, feats).T, residual.reshape(outs, chip_rows).T)  5.06 us

profile of v1, /device:TPU:1, one launch (start us, length us, event | category | flops | bytes accessed | tf_op | source)
XLA Modules:
  0.0 215.3 jit_solution(16520293380950237175)
XLA Ops:
  0.6 209.6 %shard_map.68 = (f32[4,32,2048]{2,1,0:T(8,128)}, f32[4,32,2048]{2,1,0:T(8,128)}) custom-call(s32[6]{0:T(128)} %order_ref.1, bf16[2048,2048]{1,0:T(8,128)(2,1)} %x_hbm.1, f32[2048,128]{1,0:T(8,128)} %r_hbm.1, f32[2048,128]{1,0:T(8,128)} %w_hbm.1, f32[128,2048]{1,0:T(8,128)} %bitcast.9), custom_call_target="tpu_custom_call" | custom-call | flops 6442450944 | bytes 8388608 | tf_op jit(solution)/shard_map/pallas_call | solution.py:398
  210.2 2.5 %copy.7 = f32[128,2048]{0,1:T(8,128)} copy(f32[128,2048]{1,0:T(8,128)} %bitcast.8) | data formatting | bytes 2097152 | tf_op jit(solution)/shard_map/reshape | solution.py:445
  212.7 2.5 %copy.8 = f32[128,2048]{0,1:T(8,128)} copy(f32[128,2048]{1,0:T(8,128)} %bitcast.7) | data formatting | bytes 2097152 | tf_op jit(solution)/shard_map/reshape | solution.py:445

commit v2 on v1

--- a/solution.py
+++ b/solution.py
@@ -226,7 +226,9 @@
             u, slot = self.u, self.slot
             for q in range(2):
                 self.arrived(M_AG + q, rsb.at[u, slot, q])
-            w[u] += self.own * d_buf[u, slot]
+
+        def weights(self):
+            w[self.u] += self.own * d_buf[self.u, self.slot]
 
         def change(self):
             db = d_buf[self.u, self.slot].astype(BF16)
@@ -333,6 +335,7 @@
         if edge:
             when(2, streams + 2, c.first_merge)
         when(1, starts + 1, b.gather)
+        when(2, starts + 2, c.weights)
         when(3, starts + 3, d.total)
         when(3, starts + 3, d.all_left)
         return carry

time: 215 us -> 215 us (level)
  no operation moved by 1% of the time
where the time goes in v2:
time: 215 us
  Pallas kernels  209 us (97%)
  local copies, waits for them, and re-layouts  5.06 us (2%)
    pallas_call x1, Pallas kernels, on_device(): pl.pallas_call(functools.partial(kernel, penalty), out_shape=[jax.ShapeDt...  209 us
    reshape x2, local copies, waits for them, and re-layouts, on_device(): return (weights.reshape(outs, feats).T, residual.reshape(outs, chip_rows).T)  5.06 us

profile of v2, /device:TPU:1, one launch (start us, length us, event | category | flops | bytes accessed | tf_op | source)
XLA Modules:
  0.0 214.9 jit_solution(11702143579310744493)
XLA Ops:
  0.6 209.2 %shard_map.68 = (f32[4,32,2048]{2,1,0:T(8,128)}, f32[4,32,2048]{2,1,0:T(8,128)}) custom-call(s32[6]{0:T(128)} %order_ref.1, bf16[2048,2048]{1,0:T(8,128)(2,1)} %x_hbm.1, f32[2048,128]{1,0:T(8,128)} %r_hbm.1, f32[2048,128]{1,0:T(8,128)} %w_hbm.1, f32[128,2048]{1,0:T(8,128)} %bitcast.9), custom_call_target="tpu_custom_call" | custom-call | flops 6442450944 | bytes 8388608 | tf_op jit(solution)/shard_map/pallas_call | solution.py:401
  209.9 2.5 %copy.7 = f32[128,2048]{0,1:T(8,128)} copy(f32[128,2048]{1,0:T(8,128)} %bitcast.8) | data formatting | bytes 2097152 | tf_op jit(solution)/shard_map/reshape | solution.py:448
  212.4 2.5 %copy.8 = f32[128,2048]{0,1:T(8,128)} copy(f32[128,2048]{1,0:T(8,128)} %bitcast.7) | data formatting | bytes 2097152 | tf_op jit(solution)/shard_map/reshape | solution.py:448
